TPU v7x, 128 devices: a whole 4x4x4 slice. The times are simulated.
128 devices in a mesh: src: 16 (over y, z), rcv: 8 (over x, core).
Axes of the slice: x: 4, y: 4, z: 4, core: 2. Of those that a mesh axis runs over, the one named last changes fastest.
Arguments:
- traces: bfloat16 [2048, 1024], P('src', 'rcv'), may hold values from -300 to 300, as said below
- counts: int32 [16, 8], P('src', 'rcv'), may hold values from 1 to 4, as said below
- distances: int32 [4], replicated, may hold values from -8 to 7, as said below
Outputs:
- stacks: bfloat16 [16, 4, 64, 128, 2048], P('src', None, None, None, 'rcv')
Inputs may be any that keep to these rules, and one draw needn't show every extreme that they name: `counts`: each entry is at least 1 and at most 4; both ends occur. 4 distinct block distances; -8, -1 and 7 always occur. `traces`: finite values.
All inputs are finite; a program needn't handle non-finite values.
Results may differ from a plain program's by a relative error of at most 0.0057.
Values may be sent and summed in bfloat16 or wider, within the bound.
No kernel may reach another device: no remote copies, remote signals or barrier semaphores. Data moves between devices by JAX's collectives and lax.ppermute only.
A program may use at most 384 MiB of HBM per device.

v0:
```python
import math

import jax
import jax.numpy as jnp
from jax import lax
from jax.sharding import PartitionSpec as P

LAGS = 2048
VS = 64
WIN = 32
K = 4


def toeplitz(signals, lag_block):
    signal_count, duration = signals.shape
    padded = jnp.concatenate(
        [signals, jnp.zeros((signal_count, lag_block + 1), signals.dtype)], axis=1
    )
    repeated = jnp.tile(padded, (1, lag_block))[:, : lag_block * (duration + lag_block)]
    return repeated.reshape(signal_count, lag_block, duration + lag_block)


def correlate(shifted, extended):
    columns = [jnp.einsum("iux,jx->iju", shifted, extended, preferred_element_type=jnp.float32)]
    return jnp.concatenate(columns, axis=2)


def on_device(traces, counts, distances):
    rcv_total = lax.axis_size("rcv")
    own_block = lax.axis_index("src")
    own_part = lax.axis_index("rcv")
    channels, samples = traces.shape
    lag_share = LAGS // rcv_total
    lag_block = math.gcd(lag_share, 256)
    values = traces.astype(jnp.float32)
    energy, windows = lax.psum(
        (jnp.sum(values * values, axis=1), counts[0, 0].astype(jnp.float32)), "rcv"
    )
    inverse_rms = lax.rsqrt(energy / (samples * rcv_total) + 1e-06)
    whitened = (values * inverse_rms[:, None]).astype(jnp.bfloat16)
    kept_mask = jnp.arange(samples, dtype=jnp.int32) < counts[0, 0] * WIN
    sources = jnp.where(kept_mask[None, :], whitened[:VS], jnp.zeros((), jnp.bfloat16))
    full_window, full_sources = (
        lax.all_gather(whitened, "rcv", axis=1, tiled=True),
        lax.all_gather(sources, "rcv", axis=1, tiled=True),
    )
    total_time = full_window.shape[1]
    shifted = toeplitz(full_sources, lag_block)

    def lag_slice(rows):
        padded = jnp.pad(rows, ((0, 0), (LAGS // 2, LAGS // 2)))
        return lax.dynamic_slice_in_dim(padded, own_part * lag_share, total_time + lag_share, 1)

    def add_partner(running, partner_rows, partner):
        matches = distances == partner - own_block
        target_slot = jnp.argmax(matches.astype(jnp.int32))

        def accumulate(current_stack):
            previous = lax.dynamic_index_in_dim(current_stack, target_slot, 0, keepdims=False)
            updated = previous + correlate(shifted, lag_slice(partner_rows))
            return lax.dynamic_update_index_in_dim(current_stack, updated, target_slot, 0)

        return lax.cond(jnp.any(matches), accumulate, lambda current_stack: current_stack, running)

    zero_stack = jnp.zeros((K, VS, channels, lag_share), jnp.float32)
    arrived = lax.all_gather(full_window, "src", axis=0, tiled=True)

    def add_one_block(position, running):
        partner_rows = lax.dynamic_slice_in_dim(arrived, position * channels, channels, 0)
        partner = position * channels // channels
        return add_partner(running, partner_rows, partner)

    owned_stack = lax.fori_loop(0, arrived.shape[0] // channels, add_one_block, zero_stack)
    stacked = owned_stack / jnp.sqrt(WIN * windows)
    return stacked.astype(jnp.bfloat16)[None]


def solution(mesh):
    in_specs = (P("src", "rcv"), P("src", "rcv"), P())
    out_specs = P("src", None, None, None, "rcv")
    return jax.shard_map(
        on_device, mesh=mesh, in_specs=in_specs, out_specs=out_specs, check_vma=False
    )
```

profile of v0, /device:TPU:19, one launch (start us, length us, event | category | flops | bytes accessed | tf_op | source)
XLA Modules:
  0.0 426.8 jit_solution(10466790095833608592)
XLA Ops:
  8.1 11.2 %all-reduce.2 = (f32[128]{0:T(128)S(1)}, f32[]{:T(128)}) all-reduce(f32[128]{0:T(128)S(1)} %fusion.6, f32[]{:T(128)} %bitcast.5), channel_id=1, replica_groups=mesh['src'=16,'rcv'=8] {'rcv'}, use_global_device_ids=true, to_apply=%region_1.0 | all-reduce | flops 129 | bytes 1032 | tf_op jit(solution)/shard_map/psum | solution.py:36
  20.1 15.8 %all_gather.9 = bf16[128,1024]{1,0:T(8,128)(2,1)} all-gather(bf16[128,128]{1,0:T(8,128)(2,1)S(1)} %fusion.7), channel_id=1, replica_groups=mesh['src'=16,'rcv'=8] {'rcv'}, dimensions={1}, use_global_device_ids=true | all-gather | bytes 294912 | tf_op jit(solution)/shard_map/all_gather | solution.py:44
  35.9 12.1 %all_gather.11 = bf16[64,1024]{1,0:T(8,128)(2,1)S(1)} all-gather(bf16[64,128]{1,0:T(8,128)(2,1)S(1)} %slice_select_fusion), channel_id=1, replica_groups=mesh['src'=16,'rcv'=8] {'rcv'}, dimensions={1}, use_global_device_ids=true | all-gather | bytes 147456 | tf_op jit(solution)/shard_map/all_gather | solution.py:45
  48.1 15.1 %tile.4 = bf16[64,256,1281]{2,1,0:T(8,128)(2,1)} broadcast(bf16[64,1281]{1,0:T(8,128)(2,1)S(1)} %concatenate.3), dimensions={0,2} | broadcast | bytes 42139776 | tf_op jit(solution)/shard_map/tile | solution.py:19
  63.2 97.5 %tile.10 = bf16[64,327936]{1,0:T(8,128)(2,1)} reshape(bf16[64,256,1281]{2,1,0:T(8,128)(2,1)} %tile.4) | data formatting | bytes 83951616 | tf_op jit(solution)/shard_map/tile | solution.py:19
  160.7 28.0 %slice.9 = bf16[64,327680]{1,0:T(8,128)(2,1)} slice(bf16[64,327936]{1,0:T(8,128)(2,1)} %tile.10), slice={[0:64], [0:327680]} | slice | bytes 83886080 | tf_op jit(solution)/shard_map/slice | solution.py:19
  188.7 28.7 %copy.4 = bf16[8,8,256,1280]{3,2,1,0:T(8,128)(2,1)} copy(bf16[8,8,256,1280]{3,1,2,0:T(8,128)(2,1)} %bitcast.19) | data formatting | bytes 83886080
  218.2 11.2 %broadcast_in_dim.27 = f32[4,64,128,256]{3,2,1,0:T(8,128)} broadcast(f32[]{:T(128)} %constant.142.clone.1), dimensions={} | broadcast | bytes 33554436 | tf_op jit(solution)/shard_map/broadcast_in_dim | solution.py:65
  229.4 172.5 %while.18 = (s32[]{:T(128)}, f32[4,64,128,256]{3,2,1,0:T(8,128)}, s32[]{:T(128)}, s32[4]{0:T(128)S(1)}, bf16[2048,1024]{1,0:T(8,128)(2,1)}, /*index=5*/s32[]{:T(...) while((s32[]{:T(128)}, f32[4,64,128,256]{3,2,1,0:T(8,128)}, ...), condition=%wide.region_7.8_spmd, body=%wide.region_2.7_spmd.sunk | while | flops 5370806272 | bytes 76284440 | solution.py:73
  231.4 34.9 %conditional.2 = (f32[4,64,128,256]{3,2,1,0:T(8,128)}) conditional(s32[]{:T(128)} %convert_element_type.58, f32[4,64,128,256]{3,2,1,0:T(8,128)} %get-tuple-element.333, (s32[]{:T(128)}, f32[4,64,128,256]{3,2,1,0:T(8,128)}, s32[]{:T(128)}, pred[]{:T(512)}, bf16[2048,1024]{1,0:T(8,128)(2,1)}, /*index=5*/s32[]{:T(128)}, ...), branch_computations={%region_5.5_spmd, %region_6.6_spmd} | conditional | flops 5370806272 | bytes 76284032 | solution.py:63
  233.5 7.8 %constant_dynamic-slice_fusion.1 = f32[1,64,128,256]{3,2,1,0:T(8,128)} fusion(f32[4,64,128,256]{3,2,1,0:T(8,128)} %get-tuple-element.240, s32[]{:T(128)S(6)} %select_n.39), kind=kLoop, calls=%fused_computation.6 | loop fusion | bytes 16777220 | tf_op jit(solution)/shard_map/while/body/eval_jaxpr/cond/branch_1_fun/jit(dynamic_index_in_dim)/dynamic_slice | solution.py:59
  241.3 1.0 constant_dynamic-slice_fusion
  242.3 24.0 %bitcast_dynamic-update-slice_fusion = f32[4,64,128,256]{3,2,1,0:T(8,128)} fusion(f32[4,64,128,256]{3,2,1,0:T(8,128)} %get-tuple-element.240, s32[]{:T(128)S(6)} %select_n.39, f32[1,64,128,256]{3,2,1,0:T(8,128)} %constant_dynamic-slice_fusion.1, bf16[64,256,1280]{2,1,0:T(8,128)(2,1)} %get-tuple-element.246, s32[]{:T(128)S(6)} %select_n.41, ...), kind=kOutput, calls=%fused_computation | convolution fusion | flops 5370806272 | bytes 58982408 | tf_op jit(solution)/shard_map/while/body/eval_jaxpr/cond/branch_1_fun/iux,jx->iju/dot_general | solution.py:24
  276.6 34.9 %conditional.2 = (f32[4,64,128,256]{3,2,1,0:T(8,128)}) conditional(s32[]{:T(128)} %convert_element_type.58, f32[4,64,128,256]{3,2,1,0:T(8,128)} %get-tuple-element.333, (s32[]{:T(128)}, f32[4,64,128,256]{3,2,1,0:T(8,128)}, s32[]{:T(128)}, pred[]{:T(512)}, bf16[2048,1024]{1,0:T(8,128)(2,1)}, /*index=5*/s32[]{:T(128)}, ...), branch_computations={%region_5.5_spmd, %region_6.6_spmd} | conditional | flops 5370806272 | bytes 76284032 | solution.py:63
  278.7 7.8 %constant_dynamic-slice_fusion.1 = f32[1,64,128,256]{3,2,1,0:T(8,128)} fusion(f32[4,64,128,256]{3,2,1,0:T(8,128)} %get-tuple-element.240, s32[]{:T(128)S(6)} %select_n.39), kind=kLoop, calls=%fused_computation.6 | loop fusion | bytes 16777220 | tf_op jit(solution)/shard_map/while/body/eval_jaxpr/cond/branch_1_fun/jit(dynamic_index_in_dim)/dynamic_slice | solution.py:59
  286.5 1.0 constant_dynamic-slice_fusion
  287.5 24.0 %bitcast_dynamic-update-slice_fusion = f32[4,64,128,256]{3,2,1,0:T(8,128)} fusion(f32[4,64,128,256]{3,2,1,0:T(8,128)} %get-tuple-element.240, s32[]{:T(128)S(6)} %select_n.39, f32[1,64,128,256]{3,2,1,0:T(8,128)} %constant_dynamic-slice_fusion.1, bf16[64,256,1280]{2,1,0:T(8,128)(2,1)} %get-tuple-element.246, s32[]{:T(128)S(6)} %select_n.41, ...), kind=kOutput, calls=%fused_computation | convolution fusion | flops 5370806272 | bytes 58982408 | tf_op jit(solution)/shard_map/while/body/eval_jaxpr/cond/branch_1_fun/iux,jx->iju/dot_general | solution.py:24
  315.6 34.9 %conditional.2 = (f32[4,64,128,256]{3,2,1,0:T(8,128)}) conditional(s32[]{:T(128)} %convert_element_type.58, f32[4,64,128,256]{3,2,1,0:T(8,128)} %get-tuple-element.333, (s32[]{:T(128)}, f32[4,64,128,256]{3,2,1,0:T(8,128)}, s32[]{:T(128)}, pred[]{:T(512)}, bf16[2048,1024]{1,0:T(8,128)(2,1)}, /*index=5*/s32[]{:T(128)}, ...), branch_computations={%region_5.5_spmd, %region_6.6_spmd} | conditional | flops 5370806272 | bytes 76284032 | solution.py:63
  317.7 7.8 %constant_dynamic-slice_fusion.1 = f32[1,64,128,256]{3,2,1,0:T(8,128)} fusion(f32[4,64,128,256]{3,2,1,0:T(8,128)} %get-tuple-element.240, s32[]{:T(128)S(6)} %select_n.39), kind=kLoop, calls=%fused_computation.6 | loop fusion | bytes 16777220 | tf_op jit(solution)/shard_map/while/body/eval_jaxpr/cond/branch_1_fun/jit(dynamic_index_in_dim)/dynamic_slice | solution.py:59
  326.4 24.0 %bitcast_dynamic-update-slice_fusion = f32[4,64,128,256]{3,2,1,0:T(8,128)} fusion(f32[4,64,128,256]{3,2,1,0:T(8,128)} %get-tuple-element.240, s32[]{:T(128)S(6)} %select_n.39, f32[1,64,128,256]{3,2,1,0:T(8,128)} %constant_dynamic-slice_fusion.1, bf16[64,256,1280]{2,1,0:T(8,128)(2,1)} %get-tuple-element.246, s32[]{:T(128)S(6)} %select_n.41, ...), kind=kOutput, calls=%fused_computation | convolution fusion | flops 5370806272 | bytes 58982408 | tf_op jit(solution)/shard_map/while/body/eval_jaxpr/cond/branch_1_fun/iux,jx->iju/dot_general | solution.py:24
  367.1 34.9 %conditional.2 = (f32[4,64,128,256]{3,2,1,0:T(8,128)}) conditional(s32[]{:T(128)} %convert_element_type.58, f32[4,64,128,256]{3,2,1,0:T(8,128)} %get-tuple-element.333, (s32[]{:T(128)}, f32[4,64,128,256]{3,2,1,0:T(8,128)}, s32[]{:T(128)}, pred[]{:T(512)}, bf16[2048,1024]{1,0:T(8,128)(2,1)}, /*index=5*/s32[]{:T(128)}, ...), branch_computations={%region_5.5_spmd, %region_6.6_spmd} | conditional | flops 5370806272 | bytes 76284032 | solution.py:63
  369.2 7.8 %constant_dynamic-slice_fusion.1 = f32[1,64,128,256]{3,2,1,0:T(8,128)} fusion(f32[4,64,128,256]{3,2,1,0:T(8,128)} %get-tuple-element.240, s32[]{:T(128)S(6)} %select_n.39), kind=kLoop, calls=%fused_computation.6 | loop fusion | bytes 16777220 | tf_op jit(solution)/shard_map/while/body/eval_jaxpr/cond/branch_1_fun/jit(dynamic_index_in_dim)/dynamic_slice | solution.py:59
  377.9 24.0 %bitcast_dynamic-update-slice_fusion = f32[4,64,128,256]{3,2,1,0:T(8,128)} fusion(f32[4,64,128,256]{3,2,1,0:T(8,128)} %get-tuple-element.240, s32[]{:T(128)S(6)} %select_n.39, f32[1,64,128,256]{3,2,1,0:T(8,128)} %constant_dynamic-slice_fusion.1, bf16[64,256,1280]{2,1,0:T(8,128)(2,1)} %get-tuple-element.246, s32[]{:T(128)S(6)} %select_n.41, ...), kind=kOutput, calls=%fused_computation | convolution fusion | flops 5370806272 | bytes 58982408 | tf_op jit(solution)/shard_map/while/body/eval_jaxpr/cond/branch_1_fun/iux,jx->iju/dot_general | solution.py:24
  401.9 18.0 %fusion.5 = bf16[1,4,64,128,256]{4,3,2,1,0:T(8,128)(2,1)} fusion(f32[4,64,128,256]{3,2,1,0:T(8,128)} %get-tuple-element.257, f32[]{:T(128)S(6)} %sqrt.3), kind=kLoop, calls=%fused_computation.12 | loop fusion | flops 16777216 | bytes 50331652 | tf_op jit(solution)/shard_map/broadcast_in_dim | solution.py:75
  (57 shorter events, 25.8 us)
Async XLA Ops:
  6.5 211.7 %all-gather.2.cloned.1.call-start = ((), (), s32[]{:S(2)}) async-start(), calls=%async_computation | async-start | bytes 4456448 | tf_op jit(solution)/shard_map/all_gather | solution.py:66
  217.5 11.9 %copy-start = (s32[4]{0:T(128)S(1)}, s32[4]{0:T(128)}, u32[]{:S(2)}) copy-start(s32[4]{0:T(128)} %param.9) | copy-start | bytes 52
Sparse Core Ops, SparseCore 0:
  36.0 54.6 all-gather.1
where the time goes:
time: 429 us; the launch traced here: 427 us
  local copies, waits for them, and re-layouts  216 us (50%)
  matrix products  96.1 us (22%)
  other arithmetic  41.6 us (10%)
  blocking collectives  39.1 us (9%)
  loops' own time  19.6 us (5%)
  between operations  14.8 us (3%)
    another operation x2, local copies, waits for them, and re-layouts, toeplitz(): jnp.tile(padded, (1, lag_block))[:, :lag_block * (duration + lag_block)]  113 us
    dot_general x4, matrix products, correlate(): jnp.einsum('iux,jx->iju', shifted, extended, preferred_element_type=jnp.f...  96.1 us
    dynamic_slice x4, local copies, waits for them, and re-layouts, accumulate(): lax.dynamic_index_in_dim(current_stack, target_slot, 0, keepdims=False)  31.1 us
    unnamed x3, local copies, waits for them, and re-layouts  28.7 us
    slice x1, local copies, waits for them, and re-layouts, toeplitz(): jnp.tile(padded, (1, lag_block))[:, :lag_block * (duration + lag_block)]  28 us
    broadcast_in_dim x1, other arithmetic, on_device(): return stacked.astype(jnp.bfloat16)[None]  18 us
    all_gather x1, blocking collectives, on_device(): lax.all_gather(whitened, 'rcv', axis=1, tiled=True)  15.8 us
    all_gather x1, blocking collectives, on_device(): lax.all_gather(sources, 'rcv', axis=1, tiled=True)  12.1 us
  transfers between devices with their start and end apart: 1, of which 0 were waited for; matrix products, arithmetic and copies ran while one was open for 40% of the time, Pallas kernels for 0%

commit v1 on v0

v1 whole, which is shorter than its diff:
```python
import functools

import jax
import jax.numpy as jnp
from jax import lax
from jax.experimental import pallas as pl
from jax.experimental.pallas import tpu as pltpu
from jax.sharding import PartitionSpec as P

LAGS = 2048
VS = 64
WIN = 32
K = 4
CB = 128
SEG = 128
NB = 16
TIME = 1024
SHARE = 256
SPAN = TIME + SHARE
GROUP = 4
FIXED = (-8, -1, 7)
OTHERS = (-7, -6, -5, -4, -3, -2, 0, 1, 2, 3, 4, 5, 6)


def whiten(raw):
    values = raw.astype(jnp.float32)
    energy = jnp.sum(values * values, axis=1, keepdims=True)
    return (values * lax.rsqrt(energy / TIME + 1e-06)).astype(jnp.bfloat16)


def corr_kernel(dist_ref, own_ref, counts_ref, p0, p1, p2, p3, out_ref, w_ref, v_ref, t_ref, s_ref):
    step = pl.program_id(0)

    @pl.when(step == 0)
    def _():
        for s, p in enumerate((p0, p1, p2, p3)):
            w_ref[s * CB : (s + 1) * CB, :] = whiten(p[...])
        counts = counts_ref[0:1, :].astype(jnp.float32)
        s_ref[...] = lax.rsqrt(jnp.sum(counts, axis=1, keepdims=True) * (WIN / SEG))
        lane = lax.broadcasted_iota(jnp.int32, (1, TIME), 1)
        kept = (lane % SEG).astype(jnp.float32) < counts * WIN
        sources = jnp.where(kept, whiten(own_ref[0:VS, :]).astype(jnp.float32), 0.0).astype(jnp.bfloat16)
        row = lax.broadcasted_iota(jnp.int32, (SEG, SEG), 0)
        col = lax.broadcasted_iota(jnp.int32, (SEG, SEG), 1)
        flip = jnp.where(row + col == SEG - 1, 1.0, 0.0).astype(jnp.bfloat16)
        v_ref[...] = jnp.zeros_like(v_ref)
        for e in range(8):
            part = sources[:, (7 - e) * SEG : (8 - e) * SEG]
            v_ref[:, TIME + e * SEG : TIME + (e + 1) * SEG] = jnp.dot(
                part, flip, preferred_element_type=jnp.float32
            )

    own_part = lax.axis_index("rcv")
    base = pl.multiple_of(own_part * SHARE, SHARE)
    scale = s_ref[0:1, 0:1]
    slot_of = [jnp.int32(0)] * K
    rest = jnp.int32(0)
    for k in range(K):
        fixed = jnp.bool_(False)
        for s, d in enumerate(FIXED):
            hit = dist_ref[k] == d
            slot_of[s] = jnp.where(hit, k, slot_of[s])
            fixed = jnp.logical_or(fixed, hit)
        rest = jnp.where(fixed, rest, k)
    slot_of[3] = rest
    for ii in range(GROUP):
        row = v_ref[pl.ds(step * GROUP + ii, 1), pl.ds(base, SPAN)]
        z = pltpu.roll(
            jnp.broadcast_to(row, (16, SPAN)), SPAN - 15, 1, stride=1, stride_axis=0
        ).astype(jnp.bfloat16)
        tile = t_ref.at[ii % 2]
        for g in range(TIME // 16):
            at = TIME - 16 * (g + 1)
            tile[16 * g : 16 * g + 16, :] = z[:, at : at + SHARE]
        summed = jnp.dot(w_ref[...], tile[...], preferred_element_type=jnp.float32)
        stack = (summed * scale).astype(jnp.bfloat16)
        for s in range(K):
            out_ref[slot_of[s], ii] = stack[s * CB : (s + 1) * CB]


def correlate(distances, own, counts_rows, partners):
    vmem = pl.BlockSpec((CB, TIME), lambda i: (0, 0))
    return pl.pallas_call(
        corr_kernel,
        grid=(VS // GROUP,),
        in_specs=[
            pl.BlockSpec(memory_space=pltpu.SMEM),
            vmem,
            pl.BlockSpec((16, TIME), lambda i: (0, 0)),
            vmem,
            vmem,
            vmem,
            vmem,
        ],
        out_specs=pl.BlockSpec((K, GROUP, CB, SHARE), lambda i: (0, i, 0, 0)),
        out_shape=jax.ShapeDtypeStruct((K, VS, CB, SHARE), jnp.bfloat16),
        scratch_shapes=[
            pltpu.VMEM((K * CB, TIME), jnp.bfloat16),
            pltpu.VMEM((VS, 3 * TIME), jnp.float32),
            pltpu.VMEM((2, TIME, SHARE), jnp.bfloat16),
            pltpu.VMEM((1, 1), jnp.float32),
        ],
        compiler_params=pltpu.CompilerParams(vmem_limit_bytes=48 * 2**20),
        name="corr",
    )(distances, own, counts_rows, *partners)


def shift(d):
    return [(p + d, p) for p in range(NB) if 0 <= p + d < NB]


def gather_rcv(x):
    core = lax.axis_index("rcv") % 2
    chip = lax.axis_index("rcv") // 2
    other = lax.ppermute(x, "rcv", [(s, s ^ 1) for s in range(8)])
    first = jnp.where(core == 0, x, other)
    second = jnp.where(core == 0, other, x)
    pair = jnp.concatenate([first, second], axis=1)
    turned = [pair] + [
        lax.ppermute(pair, "rcv", [((s + 2 * d) % 8, s) for s in range(8)]) for d in (1, 2, 3)
    ]
    whole = jnp.zeros((x.shape[0], TIME), x.dtype)
    for d in range(4):
        whole = lax.dynamic_update_slice(whole, turned[d], (0, (chip + d) % 4 * 256))
    return whole


def on_device(traces, counts, distances):
    rows = jnp.concatenate(
        [traces, jnp.broadcast_to(counts.astype(jnp.bfloat16), (16, SEG))], axis=0
    )
    whole = gather_rcv(rows)
    own = whole[:CB]
    partners = [lax.ppermute(own, "src", shift(d)) for d in FIXED]
    fourth = jnp.sum(distances) - sum(FIXED)
    branch = jnp.where(fourth < 0, fourth + 7, fourth + 6)
    moves = [
        (lambda y: y) if d == 0 else functools.partial(lax.ppermute, axis_name="src", perm=shift(d))
        for d in OTHERS
    ]
    partners.append(lax.switch(branch, moves, own))
    return correlate(distances, own, whole[CB:], partners)[None]


def solution(mesh):
    in_specs = (P("src", "rcv"), P("src", "rcv"), P())
    out_specs = P("src", None, None, None, "rcv")
    return jax.shard_map(
        on_device, mesh=mesh, in_specs=in_specs, out_specs=out_specs, check_vma=False
    )
```

time: 429 us -> 79.4 us (0.19)
  the two profiles are of different devices: /device:TPU:19 before, /device:TPU:16 now
where the time goes in v1:
time: 79.4 us; the launch traced here: 79.5 us
  Pallas kernels  36.7 us (46%)
  waiting for transfers between devices  21.3 us (27%)
  starting transfers between devices  15.2 us (19%)
  between operations  2.68 us (3%)
  other arithmetic  2.09 us (3%)
  local copies, waits for them, and re-layouts  1.49 us (2%)
    pallas_call x1, Pallas kernels, correlate(): pl.pallas_call(corr_kernel, grid=(VS // GROUP,), in_specs=[pl.BlockSpec(m...  36.7 us
    ppermute x1, waiting for transfers between devices, on_device(): partners.append(lax.switch(branch, moves, own))  10.8 us
    ppermute x3, starting transfers between devices, on_device(): partners = [lax.ppermute(own, 'src', shift(d)) for d in FIXED]  8.73 us
    ppermute x3, waiting for transfers between devices, gather_rcv(): lax.ppermute(pair, 'rcv', [((s + 2 * d) % 8, s) for s in range(8)])  5.43 us
    ppermute x3, starting transfers between devices, gather_rcv(): lax.ppermute(pair, 'rcv', [((s + 2 * d) % 8, s) for s in range(8)])  4.51 us
    ppermute x3, waiting for transfers between devices, on_device(): partners = [lax.ppermute(own, 'src', shift(d)) for d in FIXED]  3.82 us
    ppermute x1, starting transfers between devices, on_device(): partners.append(lax.switch(branch, moves, own))  1.92 us
  transfers between devices with their start and end apart: 8, of which 6 were waited for; matrix products, arithmetic and copies ran while one was open for 2% of the time, Pallas kernels for 0%

profile of v1, /device:TPU:16, one launch (start us, length us, event | category | flops | bytes accessed | tf_op | source)
XLA Modules:
  0.0 79.5 jit_solution(6490202141637212417)
XLA Ops:
  0.7 0.8 concatenate.6
  1.4 0.0 collective-permute-start.12
  1.4 1.2 %collective-permute-done.12 = bf16[144,128]{1,0:T(8,128)(2,1)S(1)} collective-permute-done((bf16[144,128]{1,0:T(8,128)(2,1)S(1)}, bf16[144,128]{1,0:T(8,128)(2,1)S(1)}, u32[]{:S(2)}, u32[]{:S(2)}) %collective-permute-start.12) | collective-permute-done | bytes 36896 | tf_op jit(solution)/shard_map/ppermute | solution.py:115
  2.6 0.8 broadcast_select_fusion.1
  3.5 2.8 %collective-permute-start.13 = (bf16[144,256]{1,0:T(8,128)(2,1)S(1)}, bf16[144,256]{1,0:T(8,128)(2,1)S(1)}, u32[]{:S(2)}, u32[]{:S(2)}) collective-permute-start(bf16[144,256]{1,0:T(8,128)(2,1)S(1)} %get-tuple-element.32), channel_id=1, source_target_pairs={{2,0},{3,1},{4,2},{5,3},{6,4},{7,5},{0,6},{1,7},{10,8},{11,9},{12,... | collective-permute-start | bytes 221192 | tf_op jit(solution)/shard_map/ppermute | solution.py:120
  6.3 0.8 %collective-permute-start.14 = (bf16[144,256]{1,0:T(8,128)(2,1)S(1)}, bf16[144,256]{1,0:T(8,128)(2,1)S(1)}, u32[]{:S(2)}, u32[]{:S(2)}) collective-permute-start(bf16[144,256]{1,0:T(8,128)(2,1)S(1)} %get-tuple-element.32), channel_id=1, source_target_pairs={{4,0},{5,1},{6,2},{7,3},{0,4},{1,5},{2,6},{3,7},{12,8},{13,9},{14,... | collective-permute-start | bytes 221192 | tf_op jit(solution)/shard_map/ppermute | solution.py:120
  7.1 0.9 %collective-permute-start.15 = (bf16[144,256]{1,0:T(8,128)(2,1)S(1)}, bf16[144,256]{1,0:T(8,128)(2,1)S(1)}, u32[]{:S(2)}, u32[]{:S(2)}) collective-permute-start(bf16[144,256]{1,0:T(8,128)(2,1)S(1)} %get-tuple-element.32), channel_id=1, source_target_pairs={{6,0},{7,1},{0,2},{1,3},{2,4},{3,5},{4,6},{5,7},{14,8},{15,9},{8,1... | collective-permute-start | bytes 221192 | tf_op jit(solution)/shard_map/ppermute | solution.py:120
  8.0 1.8 %collective-permute-done.13 = bf16[144,256]{1,0:T(8,128)(2,1)S(1)} collective-permute-done((bf16[144,256]{1,0:T(8,128)(2,1)S(1)}, bf16[144,256]{1,0:T(8,128)(2,1)S(1)}, u32[]{:S(2)}, u32[]{:S(2)}) %collective-permute-start.13) | collective-permute-done | bytes 73760 | tf_op jit(solution)/shard_map/ppermute | solution.py:120
  9.8 2.9 %collective-permute-done.14 = bf16[144,256]{1,0:T(8,128)(2,1)S(1)} collective-permute-done((bf16[144,256]{1,0:T(8,128)(2,1)S(1)}, bf16[144,256]{1,0:T(8,128)(2,1)S(1)}, u32[]{:S(2)}, u32[]{:S(2)}) %collective-permute-start.14) | collective-permute-done | bytes 73760 | tf_op jit(solution)/shard_map/ppermute | solution.py:120
  12.7 0.7 collective-permute-done.15
  13.5 3.6 %collective-permute-start.18 = (bf16[128,1024]{1,0:T(8,128)(2,1)S(1)}, bf16[128,1024]{1,0:T(8,128)(2,1)S(1)}, u32[]{:S(2)}, u32[]{:S(2)}) collective-permute-start(bf16[128,1024]{1,0:T(8,128)(2,1)S(1)} %slice.47.own_ref), channel_id=1, source_target_pairs={{56,0},{64,8},{72,16},{80,24},{88,32},{96,40},{104,48},{112,56},{1... | collective-permute-start | bytes 786440 | tf_op jit(solution)/shard_map/ppermute | solution.py:134
  17.1 3.8 %collective-permute-start.17 = (bf16[128,1024]{1,0:T(8,128)(2,1)S(1)}, bf16[128,1024]{1,0:T(8,128)(2,1)S(1)}, u32[]{:S(2)}, u32[]{:S(2)}) collective-permute-start(bf16[128,1024]{1,0:T(8,128)(2,1)S(1)} %slice.47.own_ref), channel_id=1, source_target_pairs={{0,8},{8,16},{16,24},{24,32},{32,40},{40,48},{48,56},{56,64},{64,7... | collective-permute-start | bytes 786440 | tf_op jit(solution)/shard_map/ppermute | solution.py:134
  20.9 1.3 %collective-permute-start.16 = (bf16[128,1024]{1,0:T(8,128)(2,1)S(1)}, bf16[128,1024]{1,0:T(8,128)(2,1)S(1)}, u32[]{:S(2)}, u32[]{:S(2)}) collective-permute-start(bf16[128,1024]{1,0:T(8,128)(2,1)S(1)} %slice.47.own_ref), channel_id=1, source_target_pairs={{0,64},{8,72},{16,80},{24,88},{32,96},{40,104},{48,112},{56,120},{... | collective-permute-start | bytes 786440 | tf_op jit(solution)/shard_map/ppermute | solution.py:134
  22.2 1.3 %reduce_sum.9 = s32[]{:T(128)} reduce(s32[4]{0:T(128)} %dist_ref.1, s32[]{:T(128)} %constant.58.clone.1), dimensions={0}, to_apply=%region_0.1 | reduce | flops 3 | bytes 24 | tf_op jit(solution)/shard_map/reduce_sum | solution.py:135
  25.5 12.8 %conditional.1 = (bf16[128,1024]{1,0:T(8,128)(2,1)}) conditional(s32[]{:T(128)} %clamp.3, bf16[128,1024]{1,0:T(8,128)(2,1)S(1)} %slice.47.own_ref, bf16[128,1024]{1,0:T(8,128)(2,1)S(1)} %slice.47.own_ref, bf16[128,1024]{1,0:T(8,128)(2,1)S(1)} %slice.47.own_ref, bf16[128,1024]{1,0:T(8,128)(2,1)S(1)} %slice.47.own_ref, ...), branch_computations={%region_1.2_spmd, %region_2.3_spmd, %region_3.4_spmd, %region_4.5_... | conditional | bytes 1048624 | solution.py:141
  25.5 1.9 %collective-permute-start = (bf16[128,1024]{1,0:T(8,128)(2,1)S(1)}, bf16[128,1024]{1,0:T(8,128)(2,1)}, u32[]{:S(2)}, u32[]{:S(2)}) collective-permute-start(bf16[128,1024]{1,0:T(8,128)(2,1)S(1)} %param), channel_id=1, source_target_pairs={{0,56},{8,64},{16,72},{24,80},{32,88},{40,96},{48,104},{56,112},{6... | collective-permute-start | bytes 786440 | tf_op jit(solution)/shard_map/cond/branch_0_fun/ppermute | solution.py:141
  27.4 10.8 %collective-permute-done = bf16[128,1024]{1,0:T(8,128)(2,1)} collective-permute-done((bf16[128,1024]{1,0:T(8,128)(2,1)S(1)}, bf16[128,1024]{1,0:T(8,128)(2,1)}, u32[]{:S(2)}, u32[]{:S(2)}) %collective-permute-start) | collective-permute-done | bytes 262176 | tf_op jit(solution)/shard_map/cond/branch_0_fun/ppermute | solution.py:141
  38.3 0.0 collective-permute-done.18.p2
  38.3 3.8 %collective-permute-done.17.p1 = bf16[128,1024]{1,0:T(8,128)(2,1)S(1)} collective-permute-done((bf16[128,1024]{1,0:T(8,128)(2,1)S(1)}, bf16[128,1024]{1,0:T(8,128)(2,1)S(1)}, u32[]{:S(2)}, u32[]{:S(2)}) %collective-permute-start.17) | collective-permute-done | bytes 262176 | tf_op jit(solution)/shard_map/ppermute | solution.py:134
  42.1 0.0 collective-permute-done.16.p0
  42.1 0.0 copy-start
  42.1 0.7 copy-done
  42.8 36.7 %corr.1 = bf16[4,64,128,256]{3,2,1,0:T(8,128)(2,1)} custom-call(s32[4]{0:T(128)S(1)} %copy-done, bf16[128,1024]{1,0:T(8,128)(2,1)S(1)} %slice.47.own_ref, bf16[16,1024]{1,0:T(8,128)(2,1)S(1)} %slice.48.counts_ref, bf16[128,1024]{1,0:T(8,128)(2,1)S(1)} %collective-permute-done.16.p0, bf16[128,1024]{1,0:T(8,128)(2,1)S(1)} %collective-permute-done.17.p1, ...), custom_call_target="tpu_custom_call" | custom-call | tf_op jit(solution)/shard_map/corr/pallas_call | solution.py:83
  (7 shorter events, 0.1 us)
Async XLA Ops:
  1.4 1.2 %collective-permute-start.12 = (bf16[144,128]{1,0:T(8,128)(2,1)S(1)}, bf16[144,128]{1,0:T(8,128)(2,1)S(1)}, u32[]{:S(2)}, u32[]{:S(2)}) collective-permute-start(bf16[144,128]{1,0:T(8,128)(2,1)S(1)} %concatenate.6), channel_id=1, source_target_pairs={{0,1},{1,0},{2,3},{3,2},{4,5},{5,4},{6,7},{7,6},{8,9},{9,8},{10,11... | collective-permute-start | bytes 110600 | tf_op jit(solution)/shard_map/ppermute | solution.py:115
  3.5 6.3 %collective-permute-start.13 = (bf16[144,256]{1,0:T(8,128)(2,1)S(1)}, bf16[144,256]{1,0:T(8,128)(2,1)S(1)}, u32[]{:S(2)}, u32[]{:S(2)}) collective-permute-start(bf16[144,256]{1,0:T(8,128)(2,1)S(1)} %get-tuple-element.32), channel_id=1, source_target_pairs={{2,0},{3,1},{4,2},{5,3},{6,4},{7,5},{0,6},{1,7},{10,8},{11,9},{12,... | collective-permute-start | bytes 221192 | tf_op jit(solution)/shard_map/ppermute | solution.py:120
  6.3 6.4 %collective-permute-start.14 = (bf16[144,256]{1,0:T(8,128)(2,1)S(1)}, bf16[144,256]{1,0:T(8,128)(2,1)S(1)}, u32[]{:S(2)}, u32[]{:S(2)}) collective-permute-start(bf16[144,256]{1,0:T(8,128)(2,1)S(1)} %get-tuple-element.32), channel_id=1, source_target_pairs={{4,0},{5,1},{6,2},{7,3},{0,4},{1,5},{2,6},{3,7},{12,8},{13,9},{14,... | collective-permute-start | bytes 221192 | tf_op jit(solution)/shard_map/ppermute | solution.py:120
  7.1 6.3 %collective-permute-start.15 = (bf16[144,256]{1,0:T(8,128)(2,1)S(1)}, bf16[144,256]{1,0:T(8,128)(2,1)S(1)}, u32[]{:S(2)}, u32[]{:S(2)}) collective-permute-start(bf16[144,256]{1,0:T(8,128)(2,1)S(1)} %get-tuple-element.32), channel_id=1, source_target_pairs={{6,0},{7,1},{0,2},{1,3},{2,4},{3,5},{4,6},{5,7},{14,8},{15,9},{8,1... | collective-permute-start | bytes 221192 | tf_op jit(solution)/shard_map/ppermute | solution.py:120
  13.5 24.8 %collective-permute-start.18 = (bf16[128,1024]{1,0:T(8,128)(2,1)S(1)}, bf16[128,1024]{1,0:T(8,128)(2,1)S(1)}, u32[]{:S(2)}, u32[]{:S(2)}) collective-permute-start(bf16[128,1024]{1,0:T(8,128)(2,1)S(1)} %slice.47.own_ref), channel_id=1, source_target_pairs={{56,0},{64,8},{72,16},{80,24},{88,32},{96,40},{104,48},{112,56},{1... | collective-permute-start | bytes 786440 | tf_op jit(solution)/shard_map/ppermute | solution.py:134
  17.1 25.0 %collective-permute-start.17 = (bf16[128,1024]{1,0:T(8,128)(2,1)S(1)}, bf16[128,1024]{1,0:T(8,128)(2,1)S(1)}, u32[]{:S(2)}, u32[]{:S(2)}) collective-permute-start(bf16[128,1024]{1,0:T(8,128)(2,1)S(1)} %slice.47.own_ref), channel_id=1, source_target_pairs={{0,8},{8,16},{16,24},{24,32},{32,40},{40,48},{48,56},{56,64},{64,7... | collective-permute-start | bytes 786440 | tf_op jit(solution)/shard_map/ppermute | solution.py:134
  20.9 21.2 %collective-permute-start.16 = (bf16[128,1024]{1,0:T(8,128)(2,1)S(1)}, bf16[128,1024]{1,0:T(8,128)(2,1)S(1)}, u32[]{:S(2)}, u32[]{:S(2)}) collective-permute-start(bf16[128,1024]{1,0:T(8,128)(2,1)S(1)} %slice.47.own_ref), channel_id=1, source_target_pairs={{0,64},{8,72},{16,80},{24,88},{32,96},{40,104},{48,112},{56,120},{... | collective-permute-start | bytes 786440 | tf_op jit(solution)/shard_map/ppermute | solution.py:134
  25.5 12.8 %collective-permute-start = (bf16[128,1024]{1,0:T(8,128)(2,1)S(1)}, bf16[128,1024]{1,0:T(8,128)(2,1)}, u32[]{:S(2)}, u32[]{:S(2)}) collective-permute-start(bf16[128,1024]{1,0:T(8,128)(2,1)S(1)} %param), channel_id=1, source_target_pairs={{0,56},{8,64},{16,72},{24,80},{32,88},{40,96},{48,104},{56,112},{6... | collective-permute-start | bytes 786440 | tf_op jit(solution)/shard_map/cond/branch_0_fun/ppermute | solution.py:141
  42.1 0.7 copy-start
